TPU v7x, 32 devices: a whole 2x2x4 slice. The times are simulated.
32 devices in a mesh: wide: 4 (over z), narrow: 8 (over y, x, core).
Axes of the slice: x: 2, y: 2, z: 4, core: 2. Of those that a mesh axis runs over, the one named last changes fastest.
Arguments:
- current_map: int32 [32, 1], replicated, may hold values from 0 to 15
- next_map: int32 [32, 1], replicated, may hold values from 0 to 15
- slot_counts: int32 [32, 2], P(('wide', 'narrow')), may hold values from 1 to 1024, as said below
- route: int32 [32768], P(('wide', 'narrow')), may hold values from 0 to 1023
- hidden_now: bfloat16 [32768, 768], P(('wide', 'narrow')), may hold values from -6 to 6
- grad_out: bfloat16 [32768, 2048], P(('wide', 'narrow')), may hold values from -0.1875 to 0.1875
- params: float32 [16, 768, 2048], P(None, 'narrow', 'wide'), may hold values from -0.21875 to 0.21875
- momentum: float32 [16, 768, 2048], P(None, 'narrow', 'wide'), may hold values from -6 to 6
- next_pool: bfloat16 [32768, 768], P(('wide', 'narrow')), may hold values from -6 to 6
Outputs:
- new_params: float32 [16, 768, 2048], P(None, 'narrow', 'wide')
- new_momentum: float32 [16, 768, 2048], P(None, 'narrow', 'wide')
- forward_out: bfloat16 [32768, 2048], P(('wide', 'narrow'))
Inputs may be any that keep to these rules, and one draw needn't show every extreme that they name: `current_map`: every expert is held by at least one slot. `next_map`: every expert is held by at least one slot. `slot_counts`: each column reaches 1024 on some slot.
All inputs are finite; a program needn't handle non-finite values.
Results may differ from a plain program's by a relative error of at most 0.0049.
Values may be sent and summed in bfloat16 or wider, within the bound.
A program may use at most 128 MiB of HBM per device.

v0:
```python
import jax
import jax.numpy as jnp
from jax import lax
from jax.sharding import PartitionSpec as P

momentum_decay = 0.9
step_size = 0.01


def local(
    current_map, next_map, slot_counts, route, hidden_now, grad_out, params, momentum, next_pool
):
    wide_count = lax.axis_size("wide")
    narrow_count = lax.axis_size("narrow")
    devices = wide_count * narrow_count
    tokens = hidden_now.shape[0]
    experts = params.shape[0]
    rows_own = params.shape[1]
    cols_own = params.shape[2]
    model_width = grad_out.shape[1]
    positions = lax.broadcasted_iota(jnp.int32, (tokens, 1), 0)
    masked = jnp.where(positions < slot_counts[0, 0], hidden_now, jnp.zeros_like(hidden_now))
    hidden_split = masked.reshape(tokens, narrow_count, rows_own)
    grad_split = grad_out.reshape(tokens, wide_count, cols_own)
    pieces = jnp.einsum(
        "tnr,twc->wnrc", hidden_split, grad_split, preferred_element_type=jnp.float32
    )
    expert_ids = lax.broadcasted_iota(jnp.int32, (experts, 1), 0)
    owner_table = (current_map[:, 0][None, :] == expert_ids).astype(jnp.float32)
    received = lax.all_to_all(
        pieces.reshape(devices, rows_own, cols_own),
        ("wide", "narrow"),
        split_axis=0,
        concat_axis=0,
        tiled=True,
    )
    column_count = received.shape[2]
    flattened = received.reshape(devices, rows_own * column_count)
    summed = jnp.dot(
        owner_table, flattened, precision=lax.Precision.HIGHEST, preferred_element_type=jnp.float32
    )
    expert_grad = summed.reshape(experts, rows_own, column_count)
    new_momentum = momentum_decay * momentum + expert_grad
    new_params = params - step_size * (expert_grad + momentum_decay * new_momentum)
    outgoing = jnp.take(new_params, next_map[:, 0], axis=0).astype(jnp.bfloat16)
    gathered = jnp.take(next_pool, route, axis=0)
    received = lax.all_to_all(outgoing, ("wide", "narrow"), split_axis=0, concat_axis=0, tiled=True)
    column_count = received.shape[2]
    arranged = received.reshape(wide_count, narrow_count, rows_own, column_count)
    arranged = arranged.transpose(1, 2, 0, 3).reshape(
        narrow_count * rows_own, wide_count * column_count
    )
    product = jnp.dot(gathered, arranged, preferred_element_type=jnp.float32)
    projected = product.reshape(tokens, wide_count, column_count)
    projected = projected.reshape(tokens, model_width)
    forward_out = jnp.where(positions < slot_counts[0, 1], projected, 0.0).astype(jnp.bfloat16)
    return (new_params, new_momentum, forward_out)


def solution(mesh):
    return jax.shard_map(
        local,
        mesh=mesh,
        in_specs=(
            P(),
            P(),
            P(("wide", "narrow"), None),
            P(("wide", "narrow")),
            P(("wide", "narrow"), None),
            P(("wide", "narrow"), None),
            P(None, "narrow", "wide"),
            P(None, "narrow", "wide"),
            P(("wide", "narrow"), None),
        ),
        out_specs=(
            P(None, "narrow", "wide"),
            P(None, "narrow", "wide"),
            P(("wide", "narrow"), None),
        ),
        check_vma=False,
    )
```

profile of v0, /device:TPU:0, one launch (start us, length us, event | category | flops | bytes accessed | tf_op | source)
XLA Modules:
  0.0 274.6 jit_solution(360724906633384043)
XLA Ops:
  0.6 0.0 copy-start
  0.6 1.3 fusion.16
  2.0 0.6 iota_compare_fusion.2
  2.6 1.7 copy.18
  4.4 0.1 broadcast_select_fusion
  4.5 5.2 %fusion.6 = f32[4,8,96,512]{3,2,0,1:T(8,128)S(1)} fusion(bf16[1024,8,96,1]{0,2,3,1:T(8,128)(2,1)S(1)} %bitcast.54, bf16[128,4,8,512]{3,2,1,0:T(8,128)(2,1)} %bitcast.56), kind=kOutput, calls=%fused_computation.13 | convolution fusion | flops 3221225472 | bytes 12058624 | tf_op jit(solution)/shard_map/tnr,twc->wnrc/dot_general | solution.py:25
  9.7 3.4 %copy.20 = f32[4,8,96,512]{3,2,1,0:T(8,128)} copy(f32[4,8,96,512]{3,2,0,1:T(8,128)S(1)} %fusion.6) | data formatting | bytes 12582912 | tf_op jit(solution)/shard_map/tnr,twc->wnrc/transpose | solution.py:25
  13.1 0.0 copy-start.3
  13.1 0.0 copy-start.2
  13.1 7.6 %all-to-all-start = ((f32[32,96,512]{2,1,0:T(8,128)}), f32[32,96,512]{2,1,0:T(8,128)}, u32[]{:S(2)}, u32[]{:S(2)}) async-start(f32[32,96,512]{2,1,0:T(8,128)} %bitcast.51), calls=%async_computation | async-start | bytes 12582912 | tf_op jit(solution)/shard_map/all_to_all | solution.py:30
  20.7 0.0 copy-done.3
  20.7 139.8 %all-to-all-done = f32[32,96,512]{2,1,0:T(8,128)} async-done(((f32[32,96,512]{2,1,0:T(8,128)}), f32[32,96,512]{2,1,0:T(8,128)}, u32[]{:S(2)}, u32[]{:S(2)}) %all-to-all-start) | async-done | bytes 6291488 | tf_op jit(solution)/shard_map/all_to_all | solution.py:30
  160.5 0.0 copy-done.2
  160.5 15.5 %fusion.5 = (f32[16,96,512]{2,0,1:T(8,128)}, f32[16,96,512]{2,0,1:T(8,128)S(1)}) fusion(f32[16,96,512]{2,1,0:T(8,128)} %param.16, f32[16,96,512]{2,1,0:T(8,128)} %param.15, s32[32]{0:T(128)S(1)} %bitcast.55, f32[4,8,96,512]{3,2,1,0:T(8,128)} %bitcast.21), kind=kOutput, calls=%fused_computation.12 | convolution fusion | flops 306708992 | bytes 18874496 | tf_op jit(solution)/shard_map/dot_general | solution.py:39
  176.0 3.5 %copy.26 = f32[16,96,512]{2,1,0:T(8,128)} copy(f32[16,96,512]{2,0,1:T(8,128)S(1)} %get-tuple-element.10) | data formatting | bytes 6291456
  179.5 4.4 %gather_fusion.1 = bf16[32,96,512]{2,1,0:T(8,128)(2,1)} fusion(f32[16,96,512]{2,1,0:T(8,128)} %copy.26, s32[1024]{0:T(1024)S(1)} %pad_clamp_fusion), kind=kCustom, calls=%fused_computation.1 | custom fusion | bytes 6291584 | tf_op jit(solution)/shard_map/jit(_take)/gather | solution.py:45
  183.9 4.7 %select_convert_fusion.1 = bf16[32,96,512]{2,1,0:T(8,128)(2,1)} fusion(bf16[32,96,512]{2,1,0:T(8,128)(2,1)} %gather_fusion.1, pred[32]{0:T(512)(128)(4,1)S(1)} %and_bitcast_fusion), kind=kLoop, calls=%fused_computation.6 | loop fusion | flops 1572864 | bytes 6291488 | tf_op jit(solution)/shard_map/convert_element_type | solution.py:45
  188.7 0.0 copy-start.1
  188.7 3.7 %all-to-all-start.1 = ((bf16[32,96,512]{2,1,0:T(8,128)(2,1)}), bf16[32,96,512]{2,1,0:T(8,128)(2,1)}, u32[]{:S(2)}, u32[]{:S(2)}) async-start(bf16[32,96,512]{2,1,0:T(8,128)(2,1)} %select_convert_fusion.1), calls=%async_computation.1 | async-start | bytes 6291456 | tf_op jit(solution)/shard_map/all_to_all | solution.py:47
  192.4 0.0 copy-done.1
  192.4 0.0 copy-done
  192.4 4.0 %gather_fusion = bf16[1024,768]{1,0:T(8,128)(2,1)S(1)} fusion(bf16[1024,768]{1,0:T(8,128)(2,1)S(1)} %copy-done, s32[1024]{0:T(1024)S(1)} %fusion.13), kind=kCustom, calls=%fused_computation | custom fusion | bytes 3149824 | tf_op jit(solution)/shard_map/jit(_take)/gather | solution.py:46
  196.4 0.6 iota_compare_fusion.1
  197.0 5.4 %copy.27 = f32[16,96,512]{2,1,0:T(8,128)} copy(f32[16,96,512]{2,0,1:T(8,128)} %get-tuple-element.9) | data formatting | bytes 6291456
  202.3 61.5 %all-to-all-done.1 = bf16[32,96,512]{2,1,0:T(8,128)(2,1)} async-done(((bf16[32,96,512]{2,1,0:T(8,128)(2,1)}), bf16[32,96,512]{2,1,0:T(8,128)(2,1)}, u32[]{:S(2)}, u32[]{:S(2)}) %all-to-all-start.1) | async-done | bytes 3145760 | tf_op jit(solution)/shard_map/all_to_all | solution.py:47
  263.8 4.3 %copy.25 = bf16[4,8,96,512]{3,0,2,1:T(4,128)(2,1)S(1)} copy(bf16[4,8,96,512]{3,2,1,0:T(8,128)(2,1)} %bitcast.13) | data formatting | bytes 6291456 | tf_op jit(solution)/shard_map/reshape | solution.py:49
  268.2 1.0 copy.32
  269.2 5.5 %select_convert_fusion = bf16[1024,2048]{1,0:T(8,128)(2,1)} fusion(pred[1024]{0:T(1024)(128)(4,1)S(1)} %get-tuple-element.13, bf16[768,2048]{1,0:T(8,128)(2,1)S(1)} %bitcast.53, bf16[1024,768]{1,0:T(8,128)(2,1)S(1)} %gather_fusion, pred[1024]{0:T(1024)(128)(4,1)S(1)} %get-tuple-element.14), kind=kOutput, calls=%fused_computation.2 | convolution fusion | flops 3226206208 | bytes 8914944 | tf_op jit(solution)/shard_map/dot_general | solution.py:53
  (4 shorter events, 0.0 us)
Async XLA Ops:
  0.6 191.8 %copy-start = (bf16[1024,768]{1,0:T(8,128)(2,1)S(1)}, bf16[1024,768]{1,0:T(8,128)(2,1)}, u32[]{:S(2)}) copy-start(bf16[1024,768]{1,0:T(8,128)(2,1)} %param.17) | copy-start | bytes 4718596
  13.1 7.6 %copy-start.3 = (s32[32,1]{0,1:T(1,128)S(1)}, s32[32,1]{0,1:T(1,128)}, u32[]{:S(2)}) copy-start(s32[32,1]{0,1:T(1,128)} %param.10) | copy-start | bytes 388
  13.1 147.5 %copy-start.2 = (s32[32,1]{0,1:T(1,128)S(1)}, s32[32,1]{0,1:T(1,128)}, u32[]{:S(2)}) copy-start(s32[32,1]{0,1:T(1,128)} %param.9) | copy-start | bytes 388
  13.1 147.4 %all-to-all-start = ((f32[32,96,512]{2,1,0:T(8,128)}), f32[32,96,512]{2,1,0:T(8,128)}, u32[]{:S(2)}, u32[]{:S(2)}) async-start(f32[32,96,512]{2,1,0:T(8,128)} %bitcast.51), calls=%async_computation | async-start | bytes 12582912 | tf_op jit(solution)/shard_map/all_to_all | solution.py:30
  188.7 3.7 %copy-start.1 = (s32[1024]{0:T(1024)S(1)}, s32[1024]{0:T(1024)}, u32[]{:S(2)}) copy-start(s32[1024]{0:T(1024)} %param.12) | copy-start | bytes 12292
  188.7 75.2 %all-to-all-start.1 = ((bf16[32,96,512]{2,1,0:T(8,128)(2,1)}), bf16[32,96,512]{2,1,0:T(8,128)(2,1)}, u32[]{:S(2)}, u32[]{:S(2)}) async-start(bf16[32,96,512]{2,1,0:T(8,128)(2,1)} %select_convert_fusion.1), calls=%async_computation.1 | async-start | bytes 6291456 | tf_op jit(solution)/shard_map/all_to_all | solution.py:47
where the time goes:
time: 275 us
  waiting for transfers between devices  201 us (73%)
  local copies, waits for them, and re-layouts  29.1 us (11%)
  matrix products  26.2 us (10%)
  starting transfers between devices  11.3 us (4%)
  other arithmetic  6.08 us (2%)
    all_to_all x1, waiting for transfers between devices, local(): lax.all_to_all(pieces.reshape(devices, rows_own, cols_own), ('wide', 'nar...  140 us
    all_to_all x1, waiting for transfers between devices, local(): lax.all_to_all(outgoing, ('wide', 'narrow'), split_axis=0, concat_axis=0,...  61.5 us
    dot_general x1, matrix products, local(): jnp.dot(owner_table, flattened, precision=lax.Precision.HIGHEST, preferre...  15.5 us
    unnamed x12, local copies, waits for them, and re-layouts  11.6 us
    all_to_all x1, starting transfers between devices, local(): lax.all_to_all(pieces.reshape(devices, rows_own, cols_own), ('wide', 'nar...  7.59 us
  transfers between devices with their start and end apart: 2, of which 2 were waited for; matrix products, arithmetic and copies ran while one was open for 4% of the time, Pallas kernels for 0%

commit v1 on v0

v1 whole, which is shorter than its diff:
```python
import functools

import jax
import jax.numpy as jnp
from jax import lax
from jax.experimental import pallas as pl
from jax.experimental.pallas import tpu as pltpu
from jax.sharding import PartitionSpec as P

momentum_decay = 0.9
step_size = 0.01
AXES = ("wide", "narrow")
VMEM_LIMIT = 48 * 1024 * 1024


def grad_kernel(counts, hidden, grad, out, masked):
    @pl.when(pl.program_id(0) == 0)
    def _():
        rows = lax.broadcasted_iota(jnp.int32, hidden.shape, 0)
        masked[...] = jnp.where(rows < counts[0, 0], hidden[...], jnp.zeros_like(hidden))

    out[0] = lax.dot_general(
        masked[...], grad[...], (((0,), (0,)), ((), ())), preferred_element_type=jnp.float32
    ).astype(out.dtype)


def grad_chunk(counts, hidden, grad, wide_count, width, chunk, chunks):
    tokens, hidden_width = hidden.shape
    return pl.pallas_call(
        grad_kernel,
        grid=(wide_count,),
        in_specs=[
            pl.BlockSpec(memory_space=pltpu.SMEM),
            pl.BlockSpec((tokens, hidden_width), lambda w: (0, 0)),
            pl.BlockSpec((tokens, width), lambda w: (0, w * chunks + chunk)),
        ],
        out_specs=pl.BlockSpec((1, hidden_width, width), lambda w: (w, 0, 0)),
        out_shape=jax.ShapeDtypeStruct((wide_count, hidden_width, width), jnp.bfloat16),
        scratch_shapes=[pltpu.VMEM((tokens, hidden_width), jnp.bfloat16)],
        compiler_params=pltpu.CompilerParams(vmem_limit_bytes=VMEM_LIMIT),
        cost_estimate=pl.CostEstimate(
            flops=2 * tokens * hidden_width * width * wide_count,
            bytes_accessed=2 * (tokens * hidden_width + (tokens + hidden_width) * width * wide_count),
            transcendentals=0,
        ),
        name="slot_grad",
    )(counts, hidden, grad)


def update_kernel(first, current_map, next_map, received, params, momentum, *rest):
    new_params, new_momentum, outgoing, total = rest if first else rest[2:]
    slots = received.shape[0]
    total[...] = jnp.zeros_like(total)

    def add(s, carry):
        e = current_map[s]
        total[e] = total[e] + received[s].astype(jnp.float32)
        return carry

    lax.fori_loop(0, slots, add, 0)
    grad = total[...]
    moved = momentum_decay * momentum[...] + grad
    new_momentum[...] = moved
    new_params[...] = params[...] - step_size * (grad + momentum_decay * moved)

    def pick(s, carry):
        outgoing[s] = new_params[next_map[s]].astype(outgoing.dtype)
        return carry

    lax.fori_loop(0, slots, pick, 0)


def update_chunk(current_map, next_map, received, params, momentum, before, chunk):
    slots, rows, width = received.shape
    experts = params.shape[0]
    step = rows // 2 if rows % 32 == 0 else rows
    state = pl.BlockSpec((experts, step, width), lambda r, *_: (0, r, chunk))
    block = pl.BlockSpec((slots, step, width), lambda r, *_: (0, r, 0))
    first = before is None
    return pl.pallas_call(
        functools.partial(update_kernel, first),
        grid_spec=pltpu.PrefetchScalarGridSpec(
            num_scalar_prefetch=2,
            grid=(rows // step,),
            in_specs=[block, state, state] + ([] if first else [pl.BlockSpec(memory_space=pl.ANY)] * 2),
            out_specs=[state, state, block],
            scratch_shapes=[pltpu.VMEM((experts, step, width), jnp.float32)],
        ),
        out_shape=[
            jax.ShapeDtypeStruct(params.shape, jnp.float32),
            jax.ShapeDtypeStruct(params.shape, jnp.float32),
            jax.ShapeDtypeStruct(received.shape, jnp.bfloat16),
        ],
        input_output_aliases={} if first else {5: 0, 6: 1},
        compiler_params=pltpu.CompilerParams(vmem_limit_bytes=VMEM_LIMIT),
        cost_estimate=pl.CostEstimate(
            flops=8 * slots * rows * width,
            bytes_accessed=(4 * slots + 16 * experts) * rows * width,
            transcendentals=0,
        ),
        name="momentum_step",
    )(current_map, next_map, received, params, momentum, *([] if first else before))


def forward_kernel(first, counts, rows, weight, *rest):
    out = rest[-1]
    product = jnp.dot(rows[...], weight[0], preferred_element_type=jnp.float32)
    position = lax.broadcasted_iota(jnp.int32, product.shape, 0)
    out[...] = jnp.where(position < counts[0, 1], product, 0.0).astype(out.dtype)


def forward_chunk(counts, rows, weight, before, chunk, chunks):
    wide_count, hidden_width, width = weight.shape
    tokens = rows.shape[0]
    first = before is None
    return pl.pallas_call(
        functools.partial(forward_kernel, first),
        grid=(wide_count,),
        in_specs=[
            pl.BlockSpec(memory_space=pltpu.SMEM),
            pl.BlockSpec((tokens, hidden_width), lambda w: (0, 0)),
            pl.BlockSpec((1, hidden_width, width), lambda w: (w, 0, 0)),
        ] + ([] if first else [pl.BlockSpec(memory_space=pl.ANY)]),
        out_specs=pl.BlockSpec((tokens, width), lambda w: (0, w * chunks + chunk)),
        out_shape=jax.ShapeDtypeStruct((tokens, wide_count * width * chunks), jnp.bfloat16),
        input_output_aliases={} if first else {3: 0},
        compiler_params=pltpu.CompilerParams(vmem_limit_bytes=VMEM_LIMIT),
        cost_estimate=pl.CostEstimate(
            flops=2 * tokens * hidden_width * width * wide_count,
            bytes_accessed=2 * (tokens * hidden_width + (tokens + hidden_width) * width * wide_count),
            transcendentals=0,
        ),
        name="forward_product",
    )(counts, rows, weight, *([] if first else [before]))


def exchange(blocks):
    return lax.all_to_all(blocks, AXES, split_axis=0, concat_axis=0, tiled=True)


def local(
    current_map, next_map, slot_counts, route, hidden_now, grad_out, params, momentum, next_pool
):
    wide_count = lax.axis_size("wide")
    devices = wide_count * lax.axis_size("narrow")
    rows_own, cols_own = params.shape[1:]
    hidden_width = hidden_now.shape[1]
    chunks = 4 if cols_own % 512 == 0 else 1
    width = cols_own // chunks
    current_map, next_map = current_map[:, 0], next_map[:, 0]

    received = []
    for k in range(chunks):
        pieces = grad_chunk(slot_counts, hidden_now, grad_out, wide_count, width, k, chunks)
        received.append(exchange(pieces.reshape(devices, rows_own, width)))
    next_rows = next_pool.at[route].get(mode="promise_in_bounds")
    state, weights = None, []
    for k in range(chunks):
        *state, outgoing = update_chunk(
            current_map, next_map, received[k], params, momentum, state, k
        )
        weights.append(exchange(outgoing).reshape(wide_count, hidden_width, width))
    out = None
    for k in range(chunks):
        out = forward_chunk(slot_counts, next_rows, weights[k], out, k, chunks)
    return state[0], state[1], out


def solution(mesh):
    return jax.shard_map(
        local,
        mesh=mesh,
        in_specs=(
            P(),
            P(),
            P(("wide", "narrow"), None),
            P(("wide", "narrow")),
            P(("wide", "narrow"), None),
            P(("wide", "narrow"), None),
            P(None, "narrow", "wide"),
            P(None, "narrow", "wide"),
            P(("wide", "narrow"), None),
        ),
        out_specs=(
            P(None, "narrow", "wide"),
            P(None, "narrow", "wide"),
            P(("wide", "narrow"), None),
        ),
        check_vma=False,
    )
```

time: 275 us -> 212 us (0.77)
  waiting for transfers between devices: 201 us -> 71.2 us
  blocking collectives: 0 us -> 48.5 us
  Pallas kernels: 0 us -> 47.6 us
  matrix products: 26.2 us -> 0 us
  starting transfers between devices: 11.3 us -> 25.9 us
  local copies, waits for them, and re-layouts: 29.1 us -> 16.4 us
  other arithmetic: 6.08 us -> 0.01 us
    all_to_all x2 -> x6, waiting for transfers between devices: 201 us -> 71.2 us  [exchange(): return lax.all_to_all(blocks, AXES, split_axis=0, concat_axis=0, tiled=True)]
    all_to_all x0 -> x2, blocking collectives: none -> 48.5 us  [exchange(): return lax.all_to_all(blocks, AXES, split_axis=0, concat_axis=0, tiled=True)]
    pallas_call x0 -> x12, Pallas kernels: none -> 47.6 us  [the longest x4 16.1 us: grad_chunk(): pl.pallas_call(grad_kernel, grid=(wide_count,), in_specs=[pl.BlockSpec(me...]
    dot_general x3 -> x0, matrix products: 26.2 us -> none  [the longest x1 15.5 us: local(): jnp.dot(owner_table, flattened, precision=lax.Precision.HIGHEST, preferre...]
    all_to_all x2 -> x6, starting transfers between devices: 11.3 us -> 25.9 us  [exchange(): return lax.all_to_all(blocks, AXES, split_axis=0, concat_axis=0, tiled=True)]
    convert_element_type x1 -> x0, other arithmetic: 4.75 us -> none  [local(): outgoing = jnp.take(new_params, next_map[:, 0], axis=0).astype(jnp.bfloat16)]
    gather x2 -> x1, local copies, waits for them, and re-layouts: 8.41 us -> 4 us  [local(): next_rows = next_pool.at[route].get(mode='promise_in_bounds')]
    reshape x1 -> x0, local copies, waits for them, and re-layouts: 4.32 us -> none  [local(): received.reshape(wide_count, narrow_count, rows_own, column_count)]
  transfers between devices with their start and end apart: 2 -> 6, of which waited for: 2 -> 6; matrix products, arithmetic and copies ran while one was open for 4% -> 2% of each run, Pallas kernels for 0% -> 19%
where the time goes in v1:
time: 212 us; the launch traced here: 210 us
  waiting for transfers between devices  71.2 us (34%)
  blocking collectives  48.5 us (23%)
  Pallas kernels  47.6 us (22%)
  starting transfers between devices  25.9 us (12%)
  local copies, waits for them, and re-layouts  16.4 us (8%)
    all_to_all x6, waiting for transfers between devices, exchange(): return lax.all_to_all(blocks, AXES, split_axis=0, concat_axis=0, tiled=True)  71.2 us
    all_to_all x2, blocking collectives, exchange(): return lax.all_to_all(blocks, AXES, split_axis=0, concat_axis=0, tiled=True)  48.5 us
    all_to_all x6, starting transfers between devices, exchange(): return lax.all_to_all(blocks, AXES, split_axis=0, concat_axis=0, tiled=True)  25.9 us
    pallas_call x4, Pallas kernels, grad_chunk(): pl.pallas_call(grad_kernel, grid=(wide_count,), in_specs=[pl.BlockSpec(me...  16.1 us
    pallas_call x4, Pallas kernels, update_chunk(): pl.pallas_call(functools.partial(update_kernel, first), grid_spec=pltpu.P...  15.8 us
    pallas_call x4, Pallas kernels, forward_chunk(): pl.pallas_call(functools.partial(forward_kernel, first), grid=(wide_count...  15.6 us
    unnamed x44, local copies, waits for them, and re-layouts  12.4 us
  transfers between devices with their start and end apart: 6, of which 6 were waited for; matrix products, arithmetic and copies ran while one was open for 2% of the time, Pallas kernels for 19%

profile of v1, /device:TPU:0, one launch (start us, length us, event | category | flops | bytes accessed | tf_op | source)
XLA Modules:
  0.0 210.4 jit_solution(16201766528390534672)
XLA Ops:
  0.6 0.0 copy-start
  0.6 0.0 copy-start.4
  0.7 1.5 copy-done.4
  2.2 0.0 copy-start.17
  2.2 0.7 copy-done.17
  2.8 0.0 copy-start.5
  2.8 4.1 %slot_grad.5 = bf16[4,768,128]{2,1,0:T(8,128)(2,1)S(1)} custom-call(s32[1,2]{1,0:T(1,128)S(1)} %copy-done.17, bf16[1024,768]{1,0:T(8,128)(2,1)S(1)} %copy-done.4, bf16[1024,2048]{1,0:T(8,128)(2,1)} %grad.7), custom_call_target="tpu_custom_call" | custom-call | flops 805306368 | bytes 3407872 | tf_op jit(solution)/shard_map/slot_grad/pallas_call | solution.py:29
  7.0 0.0 copy-start.11
  7.0 0.9 copy-done.11
  7.8 7.4 %all-to-all-start.1 = ((bf16[32,96,128]{2,1,0:T(8,128)(2,1)}), bf16[32,96,128]{2,1,0:T(8,128)(2,1)}, u32[]{:S(2)}, u32[]{:S(2)}) async-start(bf16[32,96,128]{2,1,0:T(8,128)(2,1)} %bitcast.14), calls=%async_computation.1 | async-start | bytes 1572864 | tf_op jit(solution)/shard_map/all_to_all | solution.py:138
  15.2 0.0 copy-done.5
  15.3 0.0 copy-done.18
  15.3 4.0 %slot_grad.7 = bf16[4,768,128]{2,1,0:T(8,128)(2,1)S(1)} custom-call(s32[1,2]{1,0:T(1,128)S(1)} %copy-done.18, bf16[1024,768]{1,0:T(8,128)(2,1)S(1)} %copy-done.5, bf16[1024,2048]{1,0:T(8,128)(2,1)} %grad.7), custom_call_target="tpu_custom_call" | custom-call | flops 805306368 | bytes 3407872 | tf_op jit(solution)/shard_map/slot_grad/pallas_call | solution.py:29
  19.3 0.0 copy-start.9
  19.3 0.9 copy-done.9
  20.2 15.7 %all-to-all-done.1.received = bf16[32,96,128]{2,1,0:T(8,128)(2,1)} async-done(((bf16[32,96,128]{2,1,0:T(8,128)(2,1)}), bf16[32,96,128]{2,1,0:T(8,128)(2,1)}, u32[]{:S(2)}, u32[]{:S(2)}) %all-to-all-start.1) | async-done | bytes 786464 | tf_op jit(solution)/shard_map/all_to_all | solution.py:138
  35.9 3.7 %all-to-all-start.3 = ((bf16[32,96,128]{2,1,0:T(8,128)(2,1)}), bf16[32,96,128]{2,1,0:T(8,128)(2,1)}, u32[]{:S(2)}, u32[]{:S(2)}) async-start(bf16[32,96,128]{2,1,0:T(8,128)(2,1)} %bitcast.12), calls=%async_computation.3 | async-start | bytes 1572864 | tf_op jit(solution)/shard_map/all_to_all | solution.py:138
  39.6 4.0 %slot_grad.6 = bf16[4,768,128]{2,1,0:T(8,128)(2,1)S(1)} custom-call(s32[1,2]{1,0:T(1,128)S(1)} %copy-done.18, bf16[1024,768]{1,0:T(8,128)(2,1)S(1)} %copy-done.5, bf16[1024,2048]{1,0:T(8,128)(2,1)} %grad.7), custom_call_target="tpu_custom_call" | custom-call | flops 805306368 | bytes 3407872 | tf_op jit(solution)/shard_map/slot_grad/pallas_call | solution.py:29
  43.6 0.0 copy-start.10
  43.6 0.9 copy-done.10
  44.5 15.7 %all-to-all-done.3.received = bf16[32,96,128]{2,1,0:T(8,128)(2,1)} async-done(((bf16[32,96,128]{2,1,0:T(8,128)(2,1)}), bf16[32,96,128]{2,1,0:T(8,128)(2,1)}, u32[]{:S(2)}, u32[]{:S(2)}) %all-to-all-start.3) | async-done | bytes 786464 | tf_op jit(solution)/shard_map/all_to_all | solution.py:138
  60.2 3.7 %all-to-all-start.2 = ((bf16[32,96,128]{2,1,0:T(8,128)(2,1)}), bf16[32,96,128]{2,1,0:T(8,128)(2,1)}, u32[]{:S(2)}, u32[]{:S(2)}) async-start(bf16[32,96,128]{2,1,0:T(8,128)(2,1)} %bitcast.13), calls=%async_computation.2 | async-start | bytes 1572864 | tf_op jit(solution)/shard_map/all_to_all | solution.py:138
  64.0 0.0 copy-start.19
  64.0 0.0 copy-start.20
  64.0 4.0 %slot_grad.4 = bf16[4,768,128]{2,1,0:T(8,128)(2,1)S(1)} custom-call(s32[1,2]{1,0:T(1,128)S(1)} %copy-done.18, bf16[1024,768]{1,0:T(8,128)(2,1)S(1)} %copy-done.5, bf16[1024,2048]{1,0:T(8,128)(2,1)} %grad.7), custom_call_target="tpu_custom_call" | custom-call | flops 805306368 | bytes 3407872 | tf_op jit(solution)/shard_map/slot_grad/pallas_call | solution.py:29
  68.0 0.0 copy-start.6
  68.0 0.9 copy-done.6
  68.9 15.7 %all-to-all-done.2.received = bf16[32,96,128]{2,1,0:T(8,128)(2,1)} async-done(((bf16[32,96,128]{2,1,0:T(8,128)(2,1)}), bf16[32,96,128]{2,1,0:T(8,128)(2,1)}, u32[]{:S(2)}, u32[]{:S(2)}) %all-to-all-start.2) | async-done | bytes 786464 | tf_op jit(solution)/shard_map/all_to_all | solution.py:138
  84.6 3.6 %all-to-all-start = ((bf16[32,96,128]{2,1,0:T(8,128)(2,1)}), bf16[32,96,128]{2,1,0:T(8,128)(2,1)S(1)}, u32[]{:S(2)}, u32[]{:S(2)}) async-start(bf16[32,96,128]{2,1,0:T(8,128)(2,1)} %bitcast.10), calls=%async_computation | async-start | bytes 1572864 | tf_op jit(solution)/shard_map/all_to_all | solution.py:138
  88.2 0.0 copy-done.19
  88.2 0.0 copy-done.20
  88.2 0.0 copy-start.1
  88.2 1.9 copy-done.1
  90.1 0.0 copy-start.2
  90.1 4.2 %momentum_step.4 = (f32[16,96,512]{2,1,0:T(8,128)}, f32[16,96,512]{2,1,0:T(8,128)}, bf16[32,96,128]{2,1,0:T(8,128)(2,1)S(1)}) custom-call(s32[32]{0:T(128)S(1)} %bitcast.17, s32[32]{0:T(128)S(1)} %bitcast.21, bf16[32,96,128]{2,1,0:T(8,128)(2,1)} %all-to-all-done.3.received, f32[16,96,512]{2,1,0:T(8,128)S(1)} %copy-done.1, f32[16,96,512]{2,1,0:T(8,128)} %momentum.7), custom_call_target="tpu_custom_call" | custom-call | flops 3145728 | bytes 4718592 | tf_op jit(solution)/shard_map/momentum_step/pallas_call | solution.py:80
  94.3 0.0 copy-start.14
  94.3 0.0 copy-done.2
  94.3 3.9 %momentum_step.5 = (f32[16,96,512]{2,1,0:T(8,128)}, f32[16,96,512]{2,1,0:T(8,128)}, bf16[32,96,128]{2,1,0:T(8,128)(2,1)S(1)}) custom-call(s32[32]{0:T(128)S(1)} %bitcast.18, s32[32]{0:T(128)S(1)} %bitcast.22, bf16[32,96,128]{2,1,0:T(8,128)(2,1)} %all-to-all-done.2.received, ...), custom_call_target="tpu_custom_call", output_to_operand_aliasing={{0}: (5, {}), {1}: (6, {})} | custom-call | flops 3145728 | bytes 4718592 | tf_op jit(solution)/shard_map/momentum_step/pallas_call | solution.py:80
  98.2 0.0 copy-done.14
  98.2 3.9 %momentum_step.6 = (f32[16,96,512]{2,1,0:T(8,128)}, f32[16,96,512]{2,1,0:T(8,128)}, bf16[32,96,128]{2,1,0:T(8,128)(2,1)S(1)}) custom-call(s32[32]{0:T(128)S(1)} %bitcast.19, s32[32]{0:T(128)S(1)} %bitcast.23, bf16[32,96,128]{2,1,0:T(8,128)(2,1)} %all-to-all-done.1.received, ...), custom_call_target="tpu_custom_call", output_to_operand_aliasing={{0}: (5, {}), {1}: (6, {})} | custom-call | flops 3145728 | bytes 4718592 | tf_op jit(solution)/shard_map/momentum_step/pallas_call | solution.py:80
  102.1 0.9 copy-done.16
  103.0 5.8 %all-to-all-done.received = bf16[32,96,128]{2,1,0:T(8,128)(2,1)S(1)} async-done(((bf16[32,96,128]{2,1,0:T(8,128)(2,1)}), bf16[32,96,128]{2,1,0:T(8,128)(2,1)S(1)}, u32[]{:S(2)}, u32[]{:S(2)}) %all-to-all-start) | async-done | bytes 786464 | tf_op jit(solution)/shard_map/all_to_all | solution.py:138
  108.8 24.4 %all_to_all.40 = bf16[32,96,128]{2,1,0:T(8,128)(2,1)} all-to-all(bf16[32,96,128]{2,1,0:T(8,128)(2,1)} %copy-done.16), channel_id=1, replica_groups=mesh['wide'=4,'narrow'=8] {'wide','narrow'}, dimensions={0} | all-to-all | bytes 1572864 | tf_op jit(solution)/shard_map/all_to_all | solution.py:138
  133.2 24.1 %all_to_all.41 = bf16[32,96,128]{2,1,0:T(8,128)(2,1)} all-to-all(bf16[32,96,128]{2,1,0:T(8,128)(2,1)S(1)} %get-tuple-element.25), channel_id=1, replica_groups=mesh['wide'=4,'narrow'=8] {'wide','narrow'}, dimensions={0} | all-to-all | bytes 1572864 | tf_op jit(solution)/shard_map/all_to_all | solution.py:138
  157.3 3.6 %all-to-all-start.7 = ((bf16[32,96,128]{2,1,0:T(8,128)(2,1)}), bf16[32,96,128]{2,1,0:T(8,128)(2,1)S(1)}, u32[]{:S(2)}, u32[]{:S(2)}) async-start(bf16[32,96,128]{2,1,0:T(8,128)(2,1)} %copy-done.14), calls=%async_computation.7 | async-start | bytes 1572864 | tf_op jit(solution)/shard_map/all_to_all | solution.py:138
  160.9 0.0 copy-start.3
  160.9 1.9 copy-done.3
  162.8 3.9 %momentum_step.7 = (f32[16,96,512]{2,1,0:T(8,128)}, f32[16,96,512]{2,1,0:T(8,128)}, bf16[32,96,128]{2,1,0:T(8,128)(2,1)S(1)}) custom-call(s32[32]{0:T(128)S(1)} %bitcast.20, s32[32]{0:T(128)S(1)} %bitcast.24, bf16[32,96,128]{2,1,0:T(8,128)(2,1)S(1)} %all-to-all-done.received, ...), custom_call_target="tpu_custom_call", output_to_operand_aliasing={{0}: (5, {}), {1}: (6, {})} | custom-call | flops 3145728 | bytes 4718592 | tf_op jit(solution)/shard_map/momentum_step/pallas_call | solution.py:80
  166.7 0.9 copy-done.15
  167.6 14.0 %all-to-all-done.7 = bf16[32,96,128]{2,1,0:T(8,128)(2,1)S(1)} async-done(((bf16[32,96,128]{2,1,0:T(8,128)(2,1)}), bf16[32,96,128]{2,1,0:T(8,128)(2,1)S(1)}, u32[]{:S(2)}, u32[]{:S(2)}) %all-to-all-start.7) | async-done | bytes 786464 | tf_op jit(solution)/shard_map/all_to_all | solution.py:138
  181.6 3.7 %all-to-all-start.4 = ((bf16[32,96,128]{2,1,0:T(8,128)(2,1)}), bf16[32,96,128]{2,1,0:T(8,128)(2,1)}, u32[]{:S(2)}, u32[]{:S(2)}) async-start(bf16[32,96,128]{2,1,0:T(8,128)(2,1)} %copy-done.15), calls=%async_computation.4 | async-start | bytes 1572864 | tf_op jit(solution)/shard_map/all_to_all | solution.py:138
  185.3 0.0 copy-done.7
  185.3 0.0 copy-done.21
  185.3 0.0 copy-done
  185.3 4.0 %gather_fusion = bf16[1024,768]{1,0:T(8,128)(2,1)S(1)} fusion(bf16[1024,768]{1,0:T(8,128)(2,1)S(1)} %copy-done, s32[1024]{0:T(1024)S(1)} %fusion), kind=kCustom, calls=%fused_computation | custom fusion | bytes 3149824 | tf_op jit(solution)/shard_map/gather | solution.py:156
  189.4 0.0 copy-start.8
  189.4 1.1 copy-done.8
  190.5 3.7 %forward_product.4.rest_0_ = bf16[1024,2048]{1,0:T(8,128)(2,1)} custom-call(s32[1,2]{1,0:T(1,128)S(1)} %copy-done.18, bf16[1024,768]{1,0:T(8,128)(2,1)S(1)} %gather_fusion, bf16[4,768,128]{2,1,0:T(8,128)(2,1)S(1)} %bitcast.11), custom_call_target="tpu_custom_call" | custom-call | flops 805306368 | bytes 3407872 | tf_op jit(solution)/shard_map/forward_product/pallas_call | solution.py:116
  194.2 0.0 copy-done.13
  194.2 3.7 %forward_product.5.rest_0_ = bf16[1024,2048]{1,0:T(8,128)(2,1)} custom-call(s32[1,2]{1,0:T(1,128)S(1)} %copy-done.18, bf16[1024,768]{1,0:T(8,128)(2,1)S(1)} %gather_fusion, bf16[4,768,128]{2,1,0:T(8,128)(2,1)S(1)} %bitcast.16, bf16[1024,2048]{1,0:T(8,128)(2,1)} %forward_product.4.rest_0_), custom_call_target="tpu_custom_call", output_to_operand_aliasing={{}: (3, {})} | custom-call | flops 805306368 | bytes 3407872 | tf_op jit(solution)/shard_map/forward_product/pallas_call | solution.py:116
  197.9 0.0 copy-done.12
  197.9 3.7 %forward_product.6.rest_0_ = bf16[1024,2048]{1,0:T(8,128)(2,1)} custom-call(s32[1,2]{1,0:T(1,128)S(1)} %copy-done.18, bf16[1024,768]{1,0:T(8,128)(2,1)S(1)} %gather_fusion, bf16[4,768,128]{2,1,0:T(8,128)(2,1)S(1)} %bitcast.15, bf16[1024,2048]{1,0:T(8,128)(2,1)} %forward_product.5.rest_0_), custom_call_target="tpu_custom_call", output_to_operand_aliasing={{}: (3, {})} | custom-call | flops 805306368 | bytes 3407872 | tf_op jit(solution)/shard_map/forward_product/pallas_call | solution.py:116
  201.7 4.2 %all-to-all-done.4 = bf16[32,96,128]{2,1,0:T(8,128)(2,1)} async-done(((bf16[32,96,128]{2,1,0:T(8,128)(2,1)}), bf16[32,96,128]{2,1,0:T(8,128)(2,1)}, u32[]{:S(2)}, u32[]{:S(2)}) %all-to-all-start.4) | async-done | bytes 786464 | tf_op jit(solution)/shard_map/all_to_all | solution.py:138
  205.9 4.5 %forward_product.7 = bf16[1024,2048]{1,0:T(8,128)(2,1)} custom-call(s32[1,2]{1,0:T(1,128)S(1)} %copy-done.18, bf16[1024,768]{1,0:T(8,128)(2,1)S(1)} %gather_fusion, bf16[4,768,128]{2,1,0:T(8,128)(2,1)} %bitcast.6.weight, bf16[1024,2048]{1,0:T(8,128)(2,1)} %forward_product.6.rest_0_), custom_call_target="tpu_custom_call", output_to_operand_aliasing={{}: (3, {})} | custom-call | flops 805306368 | bytes 3407872 | tf_op jit(solution)/shard_map/forward_product/pallas_call | solution.py:116
  (8 shorter events, 0.0 us)
Async XLA Ops:
  0.6 184.7 %copy-start = (bf16[1024,768]{1,0:T(8,128)(2,1)S(1)}, bf16[1024,768]{1,0:T(8,128)(2,1)}, u32[]{:S(2)}) copy-start(bf16[1024,768]{1,0:T(8,128)(2,1)} %param.17) | copy-start | bytes 4718596
  0.6 1.5 copy-start.4
  2.2 0.7 copy-start.17
  2.8 12.4 %copy-start.5 = (bf16[1024,768]{1,0:T(8,128)(2,1)S(1)}, bf16[1024,768]{1,0:T(8,128)(2,1)}, u32[]{:S(2)}) copy-start(bf16[1024,768]{1,0:T(8,128)(2,1)} %hidden.7) | copy-start | bytes 4718596
  2.8 12.4 %copy-start.18 = (s32[1,2]{1,0:T(1,128)S(1)}, s32[1,2]{1,0:T(1,128)}, u32[]{:S(2)}) copy-start(s32[1,2]{1,0:T(1,128)} %counts.15) | copy-start | bytes 28
  7.0 0.9 copy-start.11
  7.8 28.0 %all-to-all-start.1 = ((bf16[32,96,128]{2,1,0:T(8,128)(2,1)}), bf16[32,96,128]{2,1,0:T(8,128)(2,1)}, u32[]{:S(2)}, u32[]{:S(2)}) async-start(bf16[32,96,128]{2,1,0:T(8,128)(2,1)} %bitcast.14), calls=%async_computation.1 | async-start | bytes 1572864 | tf_op jit(solution)/shard_map/all_to_all | solution.py:138
  19.3 0.9 copy-start.9
  35.9 24.4 %all-to-all-start.3 = ((bf16[32,96,128]{2,1,0:T(8,128)(2,1)}), bf16[32,96,128]{2,1,0:T(8,128)(2,1)}, u32[]{:S(2)}, u32[]{:S(2)}) async-start(bf16[32,96,128]{2,1,0:T(8,128)(2,1)} %bitcast.12), calls=%async_computation.3 | async-start | bytes 1572864 | tf_op jit(solution)/shard_map/all_to_all | solution.py:138
  43.6 0.9 copy-start.10
  60.2 24.4 %all-to-all-start.2 = ((bf16[32,96,128]{2,1,0:T(8,128)(2,1)}), bf16[32,96,128]{2,1,0:T(8,128)(2,1)}, u32[]{:S(2)}, u32[]{:S(2)}) async-start(bf16[32,96,128]{2,1,0:T(8,128)(2,1)} %bitcast.13), calls=%async_computation.2 | async-start | bytes 1572864 | tf_op jit(solution)/shard_map/all_to_all | solution.py:138
  64.0 24.2 %copy-start.19 = (s32[32,1]{0,1:T(1,128)S(1)}, s32[32,1]{0,1:T(1,128)}, u32[]{:S(2)}) copy-start(s32[32,1]{0,1:T(1,128)} %param.9) | copy-start | bytes 388
  64.0 24.2 %copy-start.20 = (s32[32,1]{0,1:T(1,128)S(1)}, s32[32,1]{0,1:T(1,128)}, u32[]{:S(2)}) copy-start(s32[32,1]{0,1:T(1,128)} %param.10) | copy-start | bytes 388
  68.0 0.9 copy-start.6
  84.6 24.2 %all-to-all-start = ((bf16[32,96,128]{2,1,0:T(8,128)(2,1)}), bf16[32,96,128]{2,1,0:T(8,128)(2,1)S(1)}, u32[]{:S(2)}, u32[]{:S(2)}) async-start(bf16[32,96,128]{2,1,0:T(8,128)(2,1)} %bitcast.10), calls=%async_computation | async-start | bytes 1572864 | tf_op jit(solution)/shard_map/all_to_all | solution.py:138
  88.2 1.9 copy-start.1
  90.1 4.2 %copy-start.2 = (f32[16,96,512]{2,1,0:T(8,128)S(1)}, f32[16,96,512]{2,1,0:T(8,128)}, u32[]{:S(2)}) copy-start(f32[16,96,512]{2,1,0:T(8,128)} %params.7) | copy-start | bytes 9437188
  94.3 3.9 %copy-start.14 = (bf16[32,96,128]{2,1,0:T(8,128)(2,1)}, bf16[32,96,128]{2,1,0:T(8,128)(2,1)S(1)}, u32[]{:S(2)}) copy-start(bf16[32,96,128]{2,1,0:T(8,128)(2,1)S(1)} %get-tuple-element.26) | copy-start | bytes 2359300
  102.1 0.9 copy-start.16
  157.3 24.2 %all-to-all-start.7 = ((bf16[32,96,128]{2,1,0:T(8,128)(2,1)}), bf16[32,96,128]{2,1,0:T(8,128)(2,1)S(1)}, u32[]{:S(2)}, u32[]{:S(2)}) async-start(bf16[32,96,128]{2,1,0:T(8,128)(2,1)} %copy-done.14), calls=%async_computation.7 | async-start | bytes 1572864 | tf_op jit(solution)/shard_map/all_to_all | solution.py:138
  160.9 1.9 copy-start.3
  162.8 22.5 %copy-start.21 = (s32[1024]{0:T(1024)S(1)}, s32[1024]{0:T(1024)}, u32[]{:S(2)}) copy-start(s32[1024]{0:T(1024)} %param.12) | copy-start | bytes 12292
  166.7 0.9 copy-start.15
  181.6 3.7 %copy-start.7 = (bf16[32,96,128]{2,1,0:T(8,128)(2,1)}, bf16[32,96,128]{2,1,0:T(8,128)(2,1)S(1)}, u32[]{:S(2)}) copy-start(bf16[32,96,128]{2,1,0:T(8,128)(2,1)S(1)} %all-to-all-done.7) | copy-start | bytes 2359300
  181.6 24.4 %all-to-all-start.4 = ((bf16[32,96,128]{2,1,0:T(8,128)(2,1)}), bf16[32,96,128]{2,1,0:T(8,128)(2,1)}, u32[]{:S(2)}, u32[]{:S(2)}) async-start(bf16[32,96,128]{2,1,0:T(8,128)(2,1)} %copy-done.15), calls=%async_computation.4 | async-start | bytes 1572864 | tf_op jit(solution)/shard_map/all_to_all | solution.py:138
  189.4 1.1 copy-start.8
  190.5 3.7 %copy-start.13 = (bf16[32,96,128]{2,1,0:T(8,128)(2,1)S(1)}, bf16[32,96,128]{2,1,0:T(8,128)(2,1)}, u32[]{:S(2)}) copy-start(bf16[32,96,128]{2,1,0:T(8,128)(2,1)} %all_to_all.41) | copy-start | bytes 2359300
  194.2 3.7 %copy-start.12 = (bf16[32,96,128]{2,1,0:T(8,128)(2,1)S(1)}, bf16[32,96,128]{2,1,0:T(8,128)(2,1)}, u32[]{:S(2)}) copy-start(bf16[32,96,128]{2,1,0:T(8,128)(2,1)} %all_to_all.40) | copy-start | bytes 2359300

commit v2 on v1

--- a/solution.py
+++ b/solution.py
@@ -138,6 +138,226 @@
     return lax.all_to_all(blocks, AXES, split_axis=0, concat_axis=0, tiled=True)
 
 
+def fused_kernel(
+    chunks, wide_count, narrow_count,
+    current_map, next_map, counts, route, hidden_hbm, grad_hbm, params_hbm, momentum_hbm, pool_hbm,
+    new_params_hbm, new_momentum_hbm, out_hbm,
+    hidden, grad, params, momentum, pool, next_rows, sent, received, sent_weight, weight, out,
+    load_sem, grad_sem, send_sem, receive_sem, state_sem, out_sem,
+):
+    devices = wide_count * narrow_count
+    experts, rows, cols = params.shape
+    tokens = hidden.shape[0]
+    width = cols // chunks
+    my_wide, my_narrow = lax.axis_index("wide"), lax.axis_index("narrow")
+    me = my_wide * narrow_count + my_narrow
+    bf16 = jnp.bfloat16
+
+    def peer(j):
+        return (
+            lax.rem(my_wide + lax.rem(j, wide_count), wide_count),
+            lax.rem(my_narrow + j // wide_count, narrow_count),
+        )
+
+    def load(source, target, i):
+        copy = pltpu.make_async_copy(source, target, load_sem.at[i])
+        copy.start()
+        return copy
+
+    def load_grad(k, w):
+        return pltpu.make_async_copy(
+            grad_hbm.at[:, pl.ds(w * cols + k * width, width)],
+            grad.at[k, :, pl.ds(w * width, width)],
+            grad_sem.at[k, w],
+        )
+
+    hidden_load = load(hidden_hbm, hidden, 0)
+    for k in range(chunks):
+        for w in range(wide_count):
+            load_grad(k, w).start()
+    loads = [
+        load(params_hbm, params, 1),
+        load(momentum_hbm, momentum, 2),
+        load(pool_hbm, pool, 3),
+    ]
+
+    barrier = pltpu.get_barrier_semaphore()
+
+    def greet(j, carry):
+        pl.semaphore_signal(
+            barrier, inc=1, device_id=peer(j), device_id_type=pl.DeviceIdType.MESH
+        )
+        return carry
+
+    lax.fori_loop(1, devices, greet, 0)
+
+    def place(w, n):
+        return pl.ds(pl.multiple_of(n * rows, rows), rows), pl.ds(pl.multiple_of(w * width, width), width)
+
+    def exchange_start(source, target, sems):
+        own = pltpu.make_async_copy(source(my_wide, my_narrow), target, sems[1])
+        own.start()
+
+        def send(j, carry):
+            to = peer(j)
+            pltpu.make_async_remote_copy(
+                src_ref=source(*to),
+                dst_ref=target,
+                send_sem=sems[0],
+                recv_sem=sems[1],
+                device_id=to,
+                device_id_type=pl.DeviceIdType.MESH,
+            ).start()
+            return carry
+
+        lax.fori_loop(1, devices, send, 0)
+
+    hidden_load.wait()
+    live = lax.broadcasted_iota(jnp.int32, hidden.shape, 0) < counts[0, 0]
+    hidden[...] = jnp.where(live, hidden[...], jnp.zeros(hidden.shape, bf16))
+
+    for k in range(chunks):
+        for w in range(wide_count):
+            load_grad(k, w).wait()
+        sent[k] = lax.dot_general(
+            hidden[...], grad[k], (((0,), (0,)), ((), ())), preferred_element_type=jnp.float32
+        ).astype(bf16)
+        if k == 0:
+            pl.semaphore_wait(barrier, devices - 1)
+
+        def gradient_block(w, n, k=k):
+            across, along = place(w, n)
+            return sent.at[k, across, along]
+
+        exchange_start(
+            gradient_block, received.at[k, me], (send_sem.at[0, k], receive_sem.at[0, k])
+        )
+
+    for copy in loads:
+        copy.wait()
+    picked = lax.broadcasted_iota(jnp.int32, (tokens, tokens), 0) == route[...]
+    next_rows[...] = lax.dot_general(
+        jnp.where(picked, 1.0, 0.0).astype(bf16),
+        pool[...],
+        (((0,), (0,)), ((), ())),
+        preferred_element_type=jnp.float32,
+    ).astype(bf16)
+
+    for k in range(chunks):
+        pltpu.make_async_copy(received.at[k], received.at[k], receive_sem.at[0, k]).wait()
+        here = slice(k * width, (k + 1) * width)
+
+        def step(e, carry, k=k, here=here):
+            def add(s, total):
+                block = received[k, s].astype(jnp.float32)
+                return total + jnp.where(current_map[s, 0] == e, block, 0.0)
+
+            total = lax.fori_loop(0, devices, add, jnp.zeros((rows, width), jnp.float32), unroll=4)
+            moved = momentum_decay * momentum[e, :, here] + total
+            momentum[e, :, here] = moved
+            params[e, :, here] = params[e, :, here] - step_size * (total + momentum_decay * moved)
+            return carry
+
+        lax.fori_loop(0, experts, step, 0)
+
+        def pick(s, carry, k=k, here=here):
+            sent_weight[k, s] = params[next_map[s, 0], :, here].astype(bf16)
+            return carry
+
+        lax.fori_loop(0, devices, pick, 0)
+
+        def weight_block(w, n, k=k):
+            return sent_weight.at[k, w * narrow_count + n]
+
+        across, along = place(my_wide, my_narrow)
+        exchange_start(
+            weight_block, weight.at[k, across, along], (send_sem.at[1, k], receive_sem.at[1, k])
+        )
+    state_copies = [
+        pltpu.make_async_copy(params, new_params_hbm, state_sem.at[0]),
+        pltpu.make_async_copy(momentum, new_momentum_hbm, state_sem.at[1]),
+    ]
+    for copy in state_copies:
+        copy.start()
+
+    out_copies = []
+    for k in range(chunks):
+        pltpu.make_async_copy(weight.at[k], weight.at[k], receive_sem.at[1, k]).wait()
+        product = jnp.dot(next_rows[...], weight[k], preferred_element_type=jnp.float32)
+        position = lax.broadcasted_iota(jnp.int32, product.shape, 0)
+        out[k] = jnp.where(position < counts[0, 1], product, 0.0).astype(bf16)
+        for w in range(wide_count):
+            copy = pltpu.make_async_copy(
+                out.at[k, :, pl.ds(w * width, width)],
+                out_hbm.at[:, pl.ds(w * cols + k * width, width)],
+                out_sem.at[k, w],
+            )
+            copy.start()
+            out_copies.append(copy)
+    others = received.at[0, pl.ds(0, devices - 1)]
+    for part in range(2):
+        for k in range(chunks):
+            pltpu.make_async_copy(others, others, send_sem.at[part, k]).wait()
+    for copy in state_copies + out_copies:
+        copy.wait()
+
+
+def fused(
+    current_map, next_map, slot_counts, route, hidden_now, grad_out, params, momentum, next_pool, chunks
+):
+    wide_count, narrow_count = lax.axis_size("wide"), lax.axis_size("narrow")
+    devices = wide_count * narrow_count
+    experts, rows, cols = params.shape
+    tokens, hidden_width = hidden_now.shape
+    width = cols // chunks
+    bf16 = jnp.bfloat16
+    anywhere = pl.BlockSpec(memory_space=pl.ANY)
+    scalars = pl.BlockSpec(memory_space=pltpu.SMEM)
+    dma = pltpu.SemaphoreType.DMA
+    return pl.pallas_call(
+        functools.partial(fused_kernel, chunks, wide_count, narrow_count),
+        in_specs=[scalars] * 3 + [pl.BlockSpec(memory_space=pltpu.VMEM)] + [anywhere] * 5,
+        out_specs=[anywhere] * 3,
+        out_shape=[
+            jax.ShapeDtypeStruct(params.shape, jnp.float32),
+            jax.ShapeDtypeStruct(params.shape, jnp.float32),
+            jax.ShapeDtypeStruct(grad_out.shape, bf16),
+        ],
+        scratch_shapes=[
+            pltpu.VMEM(hidden_now.shape, bf16),
+            pltpu.VMEM((chunks, tokens, wide_count * width), bf16),
+            pltpu.VMEM(params.shape, jnp.float32),
+            pltpu.VMEM(params.shape, jnp.float32),
+            pltpu.VMEM(next_pool.shape, bf16),
+            pltpu.VMEM(next_pool.shape, bf16),
+            pltpu.VMEM((chunks, hidden_width, wide_count * width), bf16),
+            pltpu.VMEM((chunks, devices, rows, width), bf16),
+            pltpu.VMEM((chunks, devices, rows, width), bf16),
+            pltpu.VMEM((chunks, hidden_width, wide_count * width), bf16),
+            pltpu.VMEM((chunks, tokens, wide_count * width), bf16),
+            dma((4,)),
+            dma((chunks, wide_count)),
+            dma((2, chunks)),
+            dma((2, chunks)),
+            dma((2,)),
+            dma((chunks, wide_count)),
+        ],
+        compiler_params=pltpu.CompilerParams(
+            collective_id=0, has_side_effects=True, vmem_limit_bytes=60 * 1024 * 1024
+        ),
+        cost_estimate=pl.CostEstimate(
+            flops=4 * tokens * hidden_width * wide_count * cols,
+            bytes_accessed=8 * tokens * hidden_width + 4 * tokens * wide_count * cols
+            + 16 * experts * rows * cols,
+            transcendentals=0,
+        ),
+        name="exchange_and_step",
+    )(
+        current_map, next_map, slot_counts, route.reshape(1, tokens), hidden_now, grad_out, params,
+        momentum, next_pool,
+    )
+
+
 def local(
     current_map, next_map, slot_counts, route, hidden_now, grad_out, params, momentum, next_pool
 ):
@@ -147,6 +367,13 @@
     hidden_width = hidden_now.shape[1]
     chunks = 4 if cols_own % 512 == 0 else 1
     width = cols_own // chunks
+    if rows_own % 16 == 0 and width % 128 == 0:
+        return tuple(
+            fused(
+                current_map, next_map, slot_counts, route, hidden_now, grad_out, params, momentum,
+                next_pool, chunks,
+            )
+        )
     current_map, next_map = current_map[:, 0], next_map[:, 0]
 
     received = []

time: 212 us -> 160 us (0.75)
  Pallas kernels: 47.6 us -> 147 us
  waiting for transfers between devices: 71.2 us -> 0 us
  blocking collectives: 48.5 us -> 0 us
  starting transfers between devices: 25.9 us -> 0 us
  local copies, waits for them, and re-layouts: 16.4 us -> 12.1 us
    pallas_call x12 -> x1, Pallas kernels: 47.6 us -> 147 us  [fused(): pl.pallas_call(functools.partial(fused_kernel, chunks, wide_count, narrow...]
    all_to_all x6 -> x0, waiting for transfers between devices: 71.2 us -> none  [exchange(): return lax.all_to_all(blocks, AXES, split_axis=0, concat_axis=0, tiled=True)]
    all_to_all x2 -> x0, blocking collectives: 48.5 us -> none  [exchange(): return lax.all_to_all(blocks, AXES, split_axis=0, concat_axis=0, tiled=True)]
    all_to_all x6 -> x0, starting transfers between devices: 25.9 us -> none  [exchange(): return lax.all_to_all(blocks, AXES, split_axis=0, concat_axis=0, tiled=True)]
    gather x1 -> x0, local copies, waits for them, and re-layouts: 4 us -> none  [local(): next_rows = next_pool.at[route].get(mode='promise_in_bounds')]
    unnamed x44 -> x9, local copies, waits for them, and re-layouts: 12.4 us -> 12.1 us
  transfers between devices with their start and end apart: 6 -> 0, of which waited for: 6 -> 0; matrix products, arithmetic and copies ran while one was open for 2% -> 0% of each run, Pallas kernels for 19% -> 0%
where the time goes in v2:
time: 160 us
  Pallas kernels  147 us (92%)
  local copies, waits for them, and re-layouts  12.1 us (8%)
    pallas_call x1, Pallas kernels, fused(): pl.pallas_call(functools.partial(fused_kernel, chunks, wide_count, narrow...  147 us
    unnamed x9, local copies, waits for them, and re-layouts  12.1 us

profile of v2, /device:TPU:0, one launch (start us, length us, event | category | flops | bytes accessed | tf_op | source)
XLA Modules:
  0.0 159.8 jit_solution(3638630047226362609)
XLA Ops:
  0.6 1.3 copy.12.current_map
  2.0 1.3 copy.13.next_map
  3.3 147.0 %exchange_and_step.1 = (f32[16,96,512]{2,1,0:T(8,128)}, f32[16,96,512]{2,1,0:T(8,128)}, bf16[1024,2048]{1,0:T(8,128)(2,1)}) custom-call(s32[32,1]{1,0:T(8,128)} %copy.12.current_map, s32[32,1]{1,0:T(8,128)} %copy.13.next_map, s32[1,2]{1,0:T(1,128)} %counts.1, s32[1,1024]{1,0:T(1,128)} %bitcast.1, bf16[1024,768]{1,0:T(8,128)(2,1)} %hidden_hbm.1, ...), custom_call_target="tpu_custom_call" | custom-call | flops 6442450944 | bytes 27262976 | tf_op jit(solution)/shard_map/exchange_and_step/pallas_call | solution.py:317
  150.3 0.0 copy-start.1
  150.4 4.1 %copy.17 = f32[16,96,512]{2,1,0:T(8,128)} copy(f32[16,96,512]{2,1,0:T(8,128)} %get-tuple-element.6) | data formatting | bytes 6291456
  154.5 0.0 copy-done.1
  154.5 0.0 copy-start
  154.5 1.7 %copy.18 = f32[16,96,512]{2,1,0:T(8,128)} copy(f32[16,96,512]{2,1,0:T(8,128)S(1)} %copy-done.1) | data formatting | bytes 6291456
  156.1 1.7 %copy-done = bf16[1024,2048]{1,0:T(8,128)(2,1)S(1)} copy-done((bf16[1024,2048]{1,0:T(8,128)(2,1)S(1)}, bf16[1024,2048]{1,0:T(8,128)(2,1)}, u32[]{:S(2)}) %copy-start) | copy-done | bytes 4194328
  157.8 2.0 %copy.19 = bf16[1024,2048]{1,0:T(8,128)(2,1)} copy(bf16[1024,2048]{1,0:T(8,128)(2,1)S(1)} %copy-done) | data formatting | bytes 8388608
Async XLA Ops:
  150.3 4.1 %copy-start.1 = (f32[16,96,512]{2,1,0:T(8,128)S(1)}, f32[16,96,512]{2,1,0:T(8,128)}, u32[]{:S(2)}) copy-start(f32[16,96,512]{2,1,0:T(8,128)} %get-tuple-element.7) | copy-start | bytes 9437188
  154.5 3.3 %copy-start = (bf16[1024,2048]{1,0:T(8,128)(2,1)S(1)}, bf16[1024,2048]{1,0:T(8,128)(2,1)}, u32[]{:S(2)}) copy-start(bf16[1024,2048]{1,0:T(8,128)(2,1)} %get-tuple-element.8) | copy-start | bytes 12582916

commit v3 on v2

--- a/solution.py
+++ b/solution.py
@@ -11,6 +11,7 @@
 step_size = 0.01
 AXES = ("wide", "narrow")
 VMEM_LIMIT = 48 * 1024 * 1024
+FLIGHT = 2
 
 
 def grad_kernel(counts, hidden, grad, out, masked):
@@ -141,9 +142,9 @@
 def fused_kernel(
     chunks, wide_count, narrow_count,
     current_map, next_map, counts, route, hidden_hbm, grad_hbm, params_hbm, momentum_hbm, pool_hbm,
-    new_params_hbm, new_momentum_hbm, out_hbm,
-    hidden, grad, params, momentum, pool, next_rows, sent, received, sent_weight, weight, out,
-    load_sem, grad_sem, send_sem, receive_sem, state_sem, out_sem,
+    params, momentum, out,
+    hidden, grad, pool, next_rows, sent, received, sent_weight, weight,
+    load_sem, grad_sem, send_sem, receive_sem,
 ):
     devices = wide_count * narrow_count
     experts, rows, cols = params.shape
@@ -153,11 +154,17 @@
     me = my_wide * narrow_count + my_narrow
     bf16 = jnp.bfloat16
 
-    def peer(j):
-        return (
-            lax.rem(my_wide + lax.rem(j, wide_count), wide_count),
-            lax.rem(my_narrow + j // wide_count, narrow_count),
-        )
+    far_first = sorted(range(wide_count), key=lambda a: -min(a, wide_count - a))
+
+    def each_peer(act):
+        def around(b, carry):
+            for a in far_first:
+                act(lax.rem(my_wide + a, wide_count), lax.rem(my_narrow + b, narrow_count))
+            return carry
+
+        for a in far_first[:-1]:
+            act(lax.rem(my_wide + a, wide_count), my_narrow)
+        lax.fori_loop(1, narrow_count, around, 0)
 
     def load(source, target, i):
         copy = pltpu.make_async_copy(source, target, load_sem.at[i])
@@ -183,13 +190,10 @@
 
     barrier = pltpu.get_barrier_semaphore()
 
-    def greet(j, carry):
-        pl.semaphore_signal(
-            barrier, inc=1, device_id=peer(j), device_id_type=pl.DeviceIdType.MESH
-        )
-        return carry
-
-    lax.fori_loop(1, devices, greet, 0)
+    def greet(*to):
+        pl.semaphore_signal(barrier, inc=1, device_id=to, device_id_type=pl.DeviceIdType.MESH)
+
+    each_peer(greet)
 
     def place(w, n):
         return pl.ds(pl.multiple_of(n * rows, rows), rows), pl.ds(pl.multiple_of(w * width, width), width)
@@ -198,8 +202,7 @@
         own = pltpu.make_async_copy(source(my_wide, my_narrow), target, sems[1])
         own.start()
 
-        def send(j, carry):
-            to = peer(j)
+        def send(*to):
             pltpu.make_async_remote_copy(
                 src_ref=source(*to),
                 dst_ref=target,
@@ -208,49 +211,40 @@
                 device_id=to,
                 device_id_type=pl.DeviceIdType.MESH,
             ).start()
-            return carry
-
-        lax.fori_loop(1, devices, send, 0)
+
+        each_peer(send)
 
     hidden_load.wait()
     live = lax.broadcasted_iota(jnp.int32, hidden.shape, 0) < counts[0, 0]
     hidden[...] = jnp.where(live, hidden[...], jnp.zeros(hidden.shape, bf16))
 
-    for k in range(chunks):
+    others = received.at[0, pl.ds(0, devices - 1)]
+
+    def sent_out(part, k):
+        pltpu.make_async_copy(others, others, send_sem.at[part, k]).wait()
+
+    def gradient(k):
         for w in range(wide_count):
             load_grad(k, w).wait()
         sent[k] = lax.dot_general(
             hidden[...], grad[k], (((0,), (0,)), ((), ())), preferred_element_type=jnp.float32
         ).astype(bf16)
-        if k == 0:
-            pl.semaphore_wait(barrier, devices - 1)
-
-        def gradient_block(w, n, k=k):
+
+    def send_gradient(k):
+        def block(w, n):
             across, along = place(w, n)
             return sent.at[k, across, along]
 
-        exchange_start(
-            gradient_block, received.at[k, me], (send_sem.at[0, k], receive_sem.at[0, k])
-        )
-
-    for copy in loads:
-        copy.wait()
-    picked = lax.broadcasted_iota(jnp.int32, (tokens, tokens), 0) == route[...]
-    next_rows[...] = lax.dot_general(
-        jnp.where(picked, 1.0, 0.0).astype(bf16),
-        pool[...],
-        (((0,), (0,)), ((), ())),
-        preferred_element_type=jnp.float32,
-    ).astype(bf16)
-
-    for k in range(chunks):
+        exchange_start(block, received.at[k, me], (send_sem.at[0, k], receive_sem.at[0, k]))
+
+    def update(k):
         pltpu.make_async_copy(received.at[k], received.at[k], receive_sem.at[0, k]).wait()
         here = slice(k * width, (k + 1) * width)
 
-        def step(e, carry, k=k, here=here):
+        def step(e, carry):
             def add(s, total):
                 block = received[k, s].astype(jnp.float32)
-                return total + jnp.where(current_map[s, 0] == e, block, 0.0)
+                return total + jnp.where(current_map[0, s] == e, block, 0.0)
 
             total = lax.fori_loop(0, devices, add, jnp.zeros((rows, width), jnp.float32), unroll=4)
             moved = momentum_decay * momentum[e, :, here] + total
@@ -260,45 +254,89 @@
 
         lax.fori_loop(0, experts, step, 0)
 
-        def pick(s, carry, k=k, here=here):
-            sent_weight[k, s] = params[next_map[s, 0], :, here].astype(bf16)
+        def pick(s, carry):
+            sent_weight[k, s] = params[next_map[0, s], :, here].astype(bf16)
             return carry
 
         lax.fori_loop(0, devices, pick, 0)
 
-        def weight_block(w, n, k=k):
-            return sent_weight.at[k, w * narrow_count + n]
-
+    def send_weight(k):
         across, along = place(my_wide, my_narrow)
         exchange_start(
-            weight_block, weight.at[k, across, along], (send_sem.at[1, k], receive_sem.at[1, k])
+            lambda w, n: sent_weight.at[k, w * narrow_count + n],
+            weight.at[k, across, along],
+            (send_sem.at[1, k], receive_sem.at[1, k]),
         )
-    state_copies = [
-        pltpu.make_async_copy(params, new_params_hbm, state_sem.at[0]),
-        pltpu.make_async_copy(momentum, new_momentum_hbm, state_sem.at[1]),
-    ]
-    for copy in state_copies:
-        copy.start()
-
-    out_copies = []
-    for k in range(chunks):
+
+    def forward(k):
         pltpu.make_async_copy(weight.at[k], weight.at[k], receive_sem.at[1, k]).wait()
         product = jnp.dot(next_rows[...], weight[k], preferred_element_type=jnp.float32)
         position = lax.broadcasted_iota(jnp.int32, product.shape, 0)
         out[k] = jnp.where(position < counts[0, 1], product, 0.0).astype(bf16)
+
+    def gather():
+        for copy in loads:
+            copy.wait()
+        picked = lax.broadcasted_iota(jnp.int32, (tokens, tokens), 0) == route[...]
+        next_rows[...] = lax.dot_general(
+            jnp.where(picked, 1.0, 0.0).astype(bf16),
+            pool[...],
+            (((0,), (0,)), ((), ())),
+            preferred_element_type=jnp.float32,
+        ).astype(bf16)
+
+    sends = [(0, k) for k in range(chunks)] + [(1, k) for k in range(chunks)]
+
+    def issue(i):
+        if i >= FLIGHT:
+            sent_out(*sends[i - FLIGHT])
+        part, k = sends[i]
+        (send_weight if part else send_gradient)(k)
+
+    gradient(0)
+    pl.semaphore_wait(barrier, devices - 1)
+    issued = 0
+    for k in range(chunks):
+        if k:
+            gradient(k)
+        if issued < FLIGHT:
+            issue(issued)
+            issued += 1
+    gather()
+    for k in range(chunks):
+        while issued < min(len(sends), k + FLIGHT):
+            issue(issued)
+            issued += 1
+        update(k)
+    for k in range(chunks):
+        while issued < min(len(sends), chunks + k + FLIGHT):
+            issue(issued)
+            issued += 1
+        forward(k)
+    for part, k in sends[-FLIGHT:]:
+        sent_out(part, k)
+
+
+def store_kernel(
+    wide_count, params, momentum, out, new_params_hbm, new_momentum_hbm, out_hbm, state_sem, out_sem
+):
+    chunks, width = out.shape[0], out.shape[2] // wide_count
+    copies = [
+        pltpu.make_async_copy(params, new_params_hbm, state_sem.at[0]),
+        pltpu.make_async_copy(momentum, new_momentum_hbm, state_sem.at[1]),
+    ]
+    for k in range(chunks):
         for w in range(wide_count):
-            copy = pltpu.make_async_copy(
-                out.at[k, :, pl.ds(w * width, width)],
-                out_hbm.at[:, pl.ds(w * cols + k * width, width)],
-                out_sem.at[k, w],
+            copies.append(
+                pltpu.make_async_copy(
+                    out.at[k, :, pl.ds(w * width, width)],
+                    out_hbm.at[:, pl.ds((w * chunks + k) * width, width)],
+                    out_sem.at[k, w],
+                )
             )
-            copy.start()
-            out_copies.append(copy)
-    others = received.at[0, pl.ds(0, devices - 1)]
-    for part in range(2):
-        for k in range(chunks):
-            pltpu.make_async_copy(others, others, send_sem.at[part, k]).wait()
-    for copy in state_copies + out_copies:
+    for copy in copies:
+        copy.start()
+    for copy in copies:
         copy.wait()
 
 
@@ -314,48 +352,57 @@
     anywhere = pl.BlockSpec(memory_space=pl.ANY)
     scalars = pl.BlockSpec(memory_space=pltpu.SMEM)
     dma = pltpu.SemaphoreType.DMA
+    in_vmem = pl.BlockSpec(memory_space=pltpu.VMEM)
+    results = pl.pallas_call(
+        functools.partial(fused_kernel, chunks, wide_count, narrow_count),
+        in_specs=[scalars] * 3 + [in_vmem] + [anywhere] * 5,
+        out_specs=[in_vmem] * 3,
+        out_shape=[
+            pltpu.VMEM(params.shape, jnp.float32),
+            pltpu.VMEM(params.shape, jnp.float32),
+            pltpu.VMEM((chunks, tokens, wide_count * width), bf16),
+        ],
+        scratch_shapes=[
+            pltpu.VMEM(hidden_now.shape, bf16),
+            pltpu.VMEM((chunks, tokens, wide_count * width), bf16),
+            pltpu.VMEM(next_pool.shape, bf16),
+            pltpu.VMEM(next_pool.shape, bf16),
+            pltpu.VMEM((chunks, hidden_width, wide_count * width), bf16),
+            pltpu.VMEM((chunks, devices, rows, width), bf16),
+            pltpu.VMEM((chunks, devices, rows, width), bf16),
+            pltpu.VMEM((chunks, hidden_width, wide_count * width), bf16),
+            dma((4,)),
+            dma((chunks, wide_count)),
+            dma((2, chunks)),
+            dma((2, chunks)),
+        ],
+        compiler_params=pltpu.CompilerParams(
+            collective_id=0, has_side_effects=True, vmem_limit_bytes=53 * 1024 * 1024
+        ),
+        cost_estimate=pl.CostEstimate(
+            flops=4 * tokens * hidden_width * wide_count * cols,
+            bytes_accessed=8 * tokens * hidden_width + 4 * tokens * wide_count * cols
+            + 16 * experts * rows * cols,
+            transcendentals=0,
+        ),
+        name="exchange_and_step",
+    )(
+        current_map.reshape(1, devices), next_map.reshape(1, devices), slot_counts,
+        route.reshape(1, tokens), hidden_now, grad_out, params, momentum, next_pool,
+    )
     return pl.pallas_call(
-        functools.partial(fused_kernel, chunks, wide_count, narrow_count),
-        in_specs=[scalars] * 3 + [pl.BlockSpec(memory_space=pltpu.VMEM)] + [anywhere] * 5,
+        functools.partial(store_kernel, wide_count),
+        in_specs=[in_vmem] * 3,
         out_specs=[anywhere] * 3,
         out_shape=[
             jax.ShapeDtypeStruct(params.shape, jnp.float32),
             jax.ShapeDtypeStruct(params.shape, jnp.float32),
             jax.ShapeDtypeStruct(grad_out.shape, bf16),
         ],
-        scratch_shapes=[
-            pltpu.VMEM(hidden_now.shape, bf16),
-            pltpu.VMEM((chunks, tokens, wide_count * width), bf16),
-            pltpu.VMEM(params.shape, jnp.float32),
-            pltpu.VMEM(params.shape, jnp.float32),
-            pltpu.VMEM(next_pool.shape, bf16),
-            pltpu.VMEM(next_pool.shape, bf16),
-            pltpu.VMEM((chunks, hidden_width, wide_count * width), bf16),
-            pltpu.VMEM((chunks, devices, rows, width), bf16),
-            pltpu.VMEM((chunks, devices, rows, width), bf16),
-            pltpu.VMEM((chunks, hidden_width, wide_count * width), bf16),
-            pltpu.VMEM((chunks, tokens, wide_count * width), bf16),
-            dma((4,)),
-            dma((chunks, wide_count)),
-            dma((2, chunks)),
-            dma((2, chunks)),
-            dma((2,)),
-            dma((chunks, wide_count)),
-        ],
-        compiler_params=pltpu.CompilerParams(
-            collective_id=0, has_side_effects=True, vmem_limit_bytes=60 * 1024 * 1024
-        ),
-        cost_estimate=pl.CostEstimate(
-            flops=4 * tokens * hidden_width * wide_count * cols,
-            bytes_accessed=8 * tokens * hidden_width + 4 * tokens * wide_count * cols
-            + 16 * experts * rows * cols,
-            transcendentals=0,
-        ),
-        name="exchange_and_step",
-    )(
-        current_map, next_map, slot_counts, route.reshape(1, tokens), hidden_now, grad_out, params,
-        momentum, next_pool,
-    )
+        scratch_shapes=[dma((2,)), dma((chunks, wide_count))],
+        compiler_params=pltpu.CompilerParams(vmem_limit_bytes=16 * 1024 * 1024),
+        name="store_results",
+    )(*results)
 
 
 def local(

time: 160 us -> 150 us (0.938)
  local copies, waits for them, and re-layouts: 12.1 us -> 0 us
  Pallas kernels: 147 us -> 149 us
    unnamed x9 -> x0, local copies, waits for them, and re-layouts: 12.1 us -> none
    pallas_call x0 -> x1, Pallas kernels: none -> 4.17 us  [fused(): pl.pallas_call(functools.partial(store_kernel, wide_count), in_specs=[in_...]
    pallas_call x1, Pallas kernels: 147 us -> 145 us  [fused(): pl.pallas_call(functools.partial(fused_kernel, chunks, wide_count, narrow...]
where the time goes in v3:
time: 150 us
  Pallas kernels  149 us (99%)
    pallas_call x1, Pallas kernels, fused(): pl.pallas_call(functools.partial(fused_kernel, chunks, wide_count, narrow...  145 us
    pallas_call x1, Pallas kernels, fused(): pl.pallas_call(functools.partial(store_kernel, wide_count), in_specs=[in_...  4.17 us

profile of v3, /device:TPU:0, one launch (start us, length us, event | category | flops | bytes accessed | tf_op | source)
XLA Modules:
  0.0 150.1 jit_solution(7340573332145847424)
XLA Ops:
  0.6 145.3 %exchange_and_step.1 = (f32[16,96,512]{2,1,0:T(8,128)S(1)}, f32[16,96,512]{2,1,0:T(8,128)S(1)}, bf16[4,1024,512]{2,1,0:T(8,128)(2,1)S(1)}) custom-call(s32[1,32]{1,0:T(1,128)} %bitcast.4, s32[1,32]{1,0:T(1,128)} %bitcast.5, s32[1,2]{1,0:T(1,128)} %counts.1, s32[1,1024]{1,0:T(1,128)} %bitcast.3, bf16[1024,768]{1,0:T(8,128)(2,1)} %hidden_hbm.1, ...), custom_call_target="tpu_custom_call" | custom-call | flops 6442450944 | bytes 27262976 | tf_op jit(solution)/shard_map/exchange_and_step/pallas_call | solution.py:356
  146.0 4.2 %store_results.1 = (f32[16,96,512]{2,1,0:T(8,128)}, f32[16,96,512]{2,1,0:T(8,128)}, bf16[1024,2048]{1,0:T(8,128)(2,1)}) custom-call(f32[16,96,512]{2,1,0:T(8,128)S(1)} %get-tuple-element.6.params, f32[16,96,512]{2,1,0:T(8,128)S(1)} %get-tuple-element.7.momentum, bf16[4,1024,512]{2,1,0:T(8,128)(2,1)S(1)} %get-tuple-element.8.out), custom_call_target="tpu_custom_call" | custom-call | tf_op jit(solution)/shard_map/store_results/pallas_call | solution.py:393

commit v4 on v3

--- a/solution.py
+++ b/solution.py
@@ -11,7 +11,7 @@
 step_size = 0.01
 AXES = ("wide", "narrow")
 VMEM_LIMIT = 48 * 1024 * 1024
-FLIGHT = 2
+FLIGHT = 3
 
 
 def grad_kernel(counts, hidden, grad, out, masked):
@@ -139,11 +139,17 @@
     return lax.all_to_all(blocks, AXES, split_axis=0, concat_axis=0, tiled=True)
 
 
+def forward_block(counts, next_rows, weight):
+    product = jnp.dot(next_rows[...], weight, preferred_element_type=jnp.float32)
+    position = lax.broadcasted_iota(jnp.int32, product.shape, 0)
+    return jnp.where(position < counts[0, 1], product, 0.0).astype(jnp.bfloat16)
+
+
 def fused_kernel(
     chunks, wide_count, narrow_count,
     current_map, next_map, counts, route, hidden_hbm, grad_hbm, params_hbm, momentum_hbm, pool_hbm,
-    params, momentum, out,
-    hidden, grad, pool, next_rows, sent, received, sent_weight, weight,
+    params, momentum, out, next_rows, last_weight,
+    hidden, grad, pool, sent, received, sent_weight, weight,
     load_sem, grad_sem, send_sem, receive_sem,
 ):
     devices = wide_count * narrow_count
@@ -179,14 +185,8 @@
         )
 
     hidden_load = load(hidden_hbm, hidden, 0)
-    for k in range(chunks):
-        for w in range(wide_count):
-            load_grad(k, w).start()
-    loads = [
-        load(params_hbm, params, 1),
-        load(momentum_hbm, momentum, 2),
-        load(pool_hbm, pool, 3),
-    ]
+    for w in range(wide_count):
+        load_grad(0, w).start()
 
     barrier = pltpu.get_barrier_semaphore()
 
@@ -226,6 +226,9 @@
     def gradient(k):
         for w in range(wide_count):
             load_grad(k, w).wait()
+        if k + 1 < chunks:
+            for w in range(wide_count):
+                load_grad(k + 1, w).start()
         sent[k] = lax.dot_general(
             hidden[...], grad[k], (((0,), (0,)), ((), ())), preferred_element_type=jnp.float32
         ).astype(bf16)
@@ -270,9 +273,10 @@
 
     def forward(k):
         pltpu.make_async_copy(weight.at[k], weight.at[k], receive_sem.at[1, k]).wait()
-        product = jnp.dot(next_rows[...], weight[k], preferred_element_type=jnp.float32)
-        position = lax.broadcasted_iota(jnp.int32, product.shape, 0)
-        out[k] = jnp.where(position < counts[0, 1], product, 0.0).astype(bf16)
+        if k + 1 < chunks:
+            out[k] = forward_block(counts, next_rows, weight[k])
+        else:
+            last_weight[...] = weight[k]
 
     def gather():
         for copy in loads:
@@ -296,6 +300,11 @@
     gradient(0)
     pl.semaphore_wait(barrier, devices - 1)
     issued = 0
+    loads = [
+        load(params_hbm, params, 1),
+        load(momentum_hbm, momentum, 2),
+        load(pool_hbm, pool, 3),
+    ]
     for k in range(chunks):
         if k:
             gradient(k)
@@ -318,24 +327,36 @@
 
 
 def store_kernel(
-    wide_count, params, momentum, out, new_params_hbm, new_momentum_hbm, out_hbm, state_sem, out_sem
+    wide_count,
+    counts, params, momentum, out, next_rows, last_weight,
+    new_params_hbm, new_momentum_hbm, out_hbm,
+    last_out, state_sem, out_sem,
 ):
-    chunks, width = out.shape[0], out.shape[2] // wide_count
+    chunks, width = out.shape[0] + 1, out.shape[2] // wide_count
     copies = [
         pltpu.make_async_copy(params, new_params_hbm, state_sem.at[0]),
         pltpu.make_async_copy(momentum, new_momentum_hbm, state_sem.at[1]),
     ]
-    for k in range(chunks):
-        for w in range(wide_count):
-            copies.append(
-                pltpu.make_async_copy(
-                    out.at[k, :, pl.ds(w * width, width)],
-                    out_hbm.at[:, pl.ds((w * chunks + k) * width, width)],
-                    out_sem.at[k, w],
-                )
+
+    def store_out(k):
+        source = out.at[k] if k + 1 < chunks else last_out
+        return [
+            pltpu.make_async_copy(
+                source.at[:, pl.ds(w * width, width)],
+                out_hbm.at[:, pl.ds((w * chunks + k) * width, width)],
+                out_sem.at[k, w],
             )
+            for w in range(wide_count)
+        ]
+
+    for k in range(chunks - 1):
+        copies += store_out(k)
     for copy in copies:
         copy.start()
+    last_out[...] = forward_block(counts, next_rows, last_weight[...])
+    for copy in store_out(chunks - 1):
+        copy.start()
+        copies.append(copy)
     for copy in copies:
         copy.wait()
 
@@ -356,16 +377,17 @@
     results = pl.pallas_call(
         functools.partial(fused_kernel, chunks, wide_count, narrow_count),
         in_specs=[scalars] * 3 + [in_vmem] + [anywhere] * 5,
-        out_specs=[in_vmem] * 3,
+        out_specs=[in_vmem] * 5,
         out_shape=[
             pltpu.VMEM(params.shape, jnp.float32),
             pltpu.VMEM(params.shape, jnp.float32),
-            pltpu.VMEM((chunks, tokens, wide_count * width), bf16),
+            pltpu.VMEM((chunks - 1, tokens, wide_count * width), bf16),
+            pltpu.VMEM(next_pool.shape, bf16),
+            pltpu.VMEM((hidden_width, wide_count * width), bf16),
         ],
         scratch_shapes=[
             pltpu.VMEM(hidden_now.shape, bf16),
             pltpu.VMEM((chunks, tokens, wide_count * width), bf16),
-            pltpu.VMEM(next_pool.shape, bf16),
             pltpu.VMEM(next_pool.shape, bf16),
             pltpu.VMEM((chunks, hidden_width, wide_count * width), bf16),
             pltpu.VMEM((chunks, devices, rows, width), bf16),
@@ -377,7 +399,7 @@
             dma((2, chunks)),
         ],
         compiler_params=pltpu.CompilerParams(
-            collective_id=0, has_side_effects=True, vmem_limit_bytes=53 * 1024 * 1024
+            collective_id=0, has_side_effects=True, vmem_limit_bytes=52 * 1024 * 1024
         ),
         cost_estimate=pl.CostEstimate(
             flops=4 * tokens * hidden_width * wide_count * cols,
@@ -392,17 +414,21 @@
     )
     return pl.pallas_call(
         functools.partial(store_kernel, wide_count),
-        in_specs=[in_vmem] * 3,
+        in_specs=[scalars] + [in_vmem] * 5,
         out_specs=[anywhere] * 3,
         out_shape=[
             jax.ShapeDtypeStruct(params.shape, jnp.float32),
             jax.ShapeDtypeStruct(params.shape, jnp.float32),
             jax.ShapeDtypeStruct(grad_out.shape, bf16),
         ],
-        scratch_shapes=[dma((2,)), dma((chunks, wide_count))],
+        scratch_shapes=[
+            pltpu.VMEM((tokens, wide_count * width), bf16),
+            dma((2,)),
+            dma((chunks, wide_count)),
+        ],
         compiler_params=pltpu.CompilerParams(vmem_limit_bytes=16 * 1024 * 1024),
         name="store_results",
-    )(*results)
+    )(slot_counts, *results)
 
 
 def local(
@@ -414,7 +440,7 @@
     hidden_width = hidden_now.shape[1]
     chunks = 4 if cols_own % 512 == 0 else 1
     width = cols_own // chunks
-    if rows_own % 16 == 0 and width % 128 == 0:
+    if rows_own % 16 == 0 and width % 128 == 0 and chunks > 1:
         return tuple(
             fused(
                 current_map, next_map, slot_counts, route, hidden_now, grad_out, params, momentum,

time: 150 us -> 149 us (level)
  no operation moved by 1% of the time
where the time goes in v4:
time: 149 us
  Pallas kernels  149 us (100%)
    pallas_call x1, Pallas kernels, fused(): pl.pallas_call(functools.partial(fused_kernel, chunks, wide_count, narrow...  144 us
    pallas_call x1, Pallas kernels, fused(): pl.pallas_call(functools.partial(store_kernel, wide_count), in_specs=[sca...  4.66 us

profile of v4, /device:TPU:0, one launch (start us, length us, event | category | flops | bytes accessed | tf_op | source)
XLA Modules:
  0.0 149.2 jit_solution(3105756536357906078)
XLA Ops:
  0.6 0.0 copy-start
  0.6 143.9 %exchange_and_step.1 = (f32[16,96,512]{2,1,0:T(8,128)S(1)}, f32[16,96,512]{2,1,0:T(8,128)S(1)}, bf16[3,1024,512]{2,1,0:T(8,128)(2,1)S(1)}, bf16[1024,768]{1,0:T(8,128)(2,1)S(1)}, bf16[768,512]{1,0:T(8,128)(2,1)S(1)}) custom-call(s32[1,32]{1,0:T(1,128)} %bitcast.4, s32[1,32]{1,0:T(1,128)} %bitcast.5, s32[1,2]{1,0:T(1,128)} %counts.3, s32[1,1024]{1,0:T(1,128)} %bitcast.3, ...), custom_call_target="tpu_custom_call" | custom-call | flops 6442450944 | bytes 27262976 | tf_op jit(solution)/shard_map/exchange_and_step/pallas_call | solution.py:377
  144.5 0.0 copy-done
  144.5 4.7 %store_results.1 = (f32[16,96,512]{2,1,0:T(8,128)}, f32[16,96,512]{2,1,0:T(8,128)}, bf16[1024,2048]{1,0:T(8,128)(2,1)}) custom-call(s32[1,2]{1,0:T(1,128)S(1)} %copy-done, f32[16,96,512]{2,1,0:T(8,128)S(1)} %get-tuple-element.8.params, f32[16,96,512]{2,1,0:T(8,128)S(1)} %get-tuple-element.9.momentum, bf16[3,1024,512]{2,1,0:T(8,128)(2,1)S(1)} %get-tuple-element.10.out, ...), custom_call_target="tpu_custom_call" | custom-call | tf_op jit(solution)/shard_map/store_results/pallas_call | solution.py:415
Async XLA Ops:
  0.6 143.9 %copy-start = (s32[1,2]{1,0:T(1,128)S(1)}, s32[1,2]{1,0:T(1,128)}, u32[]{:S(2)}) copy-start(s32[1,2]{1,0:T(1,128)} %counts.3) | copy-start | bytes 28

commit v5 on v4

--- a/solution.py
+++ b/solution.py
@@ -196,7 +196,7 @@
     each_peer(greet)
 
     def place(w, n):
-        return pl.ds(pl.multiple_of(n * rows, rows), rows), pl.ds(pl.multiple_of(w * width, width), width)
+        return slice(n * rows, (n + 1) * rows), slice(w * width, (w + 1) * width)
 
     def exchange_start(source, target, sems):
         own = pltpu.make_async_copy(source(my_wide, my_narrow), target, sems[1])
@@ -229,16 +229,20 @@
         if k + 1 < chunks:
             for w in range(wide_count):
                 load_grad(k + 1, w).start()
-        sent[k] = lax.dot_general(
+        product = lax.dot_general(
             hidden[...], grad[k], (((0,), (0,)), ((), ())), preferred_element_type=jnp.float32
         ).astype(bf16)
+        for w in range(wide_count):
+            for n in range(narrow_count):
+                across, along = place(w, n)
+                sent[k, w * narrow_count + n] = product[across, along]
 
     def send_gradient(k):
-        def block(w, n):
-            across, along = place(w, n)
-            return sent.at[k, across, along]
-
-        exchange_start(block, received.at[k, me], (send_sem.at[0, k], receive_sem.at[0, k]))
+        exchange_start(
+            lambda w, n: sent.at[k, w * narrow_count + n],
+            received.at[k, me],
+            (send_sem.at[0, k], receive_sem.at[0, k]),
+        )
 
     def update(k):
         pltpu.make_async_copy(received.at[k], received.at[k], receive_sem.at[0, k]).wait()
@@ -264,19 +268,20 @@
         lax.fori_loop(0, devices, pick, 0)
 
     def send_weight(k):
-        across, along = place(my_wide, my_narrow)
         exchange_start(
             lambda w, n: sent_weight.at[k, w * narrow_count + n],
-            weight.at[k, across, along],
+            weight.at[k, me],
             (send_sem.at[1, k], receive_sem.at[1, k]),
         )
 
     def forward(k):
         pltpu.make_async_copy(weight.at[k], weight.at[k], receive_sem.at[1, k]).wait()
+        for w in range(wide_count):
+            for n in range(narrow_count):
+                across, along = place(w, n)
+                last_weight[across, along] = weight[k, w * narrow_count + n]
         if k + 1 < chunks:
-            out[k] = forward_block(counts, next_rows, weight[k])
-        else:
-            last_weight[...] = weight[k]
+            out[k] = forward_block(counts, next_rows, last_weight[...])
 
     def gather():
         for copy in loads:
@@ -389,10 +394,10 @@
             pltpu.VMEM(hidden_now.shape, bf16),
             pltpu.VMEM((chunks, tokens, wide_count * width), bf16),
             pltpu.VMEM(next_pool.shape, bf16),
-            pltpu.VMEM((chunks, hidden_width, wide_count * width), bf16),
             pltpu.VMEM((chunks, devices, rows, width), bf16),
             pltpu.VMEM((chunks, devices, rows, width), bf16),
-            pltpu.VMEM((chunks, hidden_width, wide_count * width), bf16),
+            pltpu.VMEM((chunks, devices, rows, width), bf16),
+            pltpu.VMEM((chunks, devices, rows, width), bf16),
             dma((4,)),
             dma((chunks, wide_count)),
             dma((2, chunks)),

time: 149 us -> 150 us (level)
  no operation moved by 1% of the time
where the time goes in v5:
time: 150 us; the launch traced here: 149 us
  Pallas kernels  149 us (99%)
    pallas_call x1, Pallas kernels, fused(): pl.pallas_call(functools.partial(fused_kernel, chunks, wide_count, narrow...  144 us
    pallas_call x1, Pallas kernels, fused(): pl.pallas_call(functools.partial(store_kernel, wide_count), in_specs=[sca...  4.66 us

profile of v5, /device:TPU:0, one launch (start us, length us, event | category | flops | bytes accessed | tf_op | source)
XLA Modules:
  0.0 149.4 jit_solution(15680771977526062968)
XLA Ops:
  0.6 0.0 copy-start
  0.6 144.0 %exchange_and_step.1 = (f32[16,96,512]{2,1,0:T(8,128)S(1)}, f32[16,96,512]{2,1,0:T(8,128)S(1)}, bf16[3,1024,512]{2,1,0:T(8,128)(2,1)S(1)}, bf16[1024,768]{1,0:T(8,128)(2,1)S(1)}, bf16[768,512]{1,0:T(8,128)(2,1)S(1)}) custom-call(s32[1,32]{1,0:T(1,128)} %bitcast.4, s32[1,32]{1,0:T(1,128)} %bitcast.5, s32[1,2]{1,0:T(1,128)} %counts.3, s32[1,1024]{1,0:T(1,128)} %bitcast.3, ...), custom_call_target="tpu_custom_call" | custom-call | flops 6442450944 | bytes 27262976 | tf_op jit(solution)/shard_map/exchange_and_step/pallas_call | solution.py:382
  144.7 0.0 copy-done
  144.7 4.7 %store_results.1 = (f32[16,96,512]{2,1,0:T(8,128)}, f32[16,96,512]{2,1,0:T(8,128)}, bf16[1024,2048]{1,0:T(8,128)(2,1)}) custom-call(s32[1,2]{1,0:T(1,128)S(1)} %copy-done, f32[16,96,512]{2,1,0:T(8,128)S(1)} %get-tuple-element.8.params, f32[16,96,512]{2,1,0:T(8,128)S(1)} %get-tuple-element.9.momentum, bf16[3,1024,512]{2,1,0:T(8,128)(2,1)S(1)} %get-tuple-element.10.out, ...), custom_call_target="tpu_custom_call" | custom-call | tf_op jit(solution)/shard_map/store_results/pallas_call | solution.py:420
Async XLA Ops:
  0.6 144.1 %copy-start = (s32[1,2]{1,0:T(1,128)S(1)}, s32[1,2]{1,0:T(1,128)}, u32[]{:S(2)}) copy-start(s32[1,2]{1,0:T(1,128)} %counts.3) | copy-start | bytes 28
